TPU v7x, 512 devices: a whole 4x8x8 slice. The times are simulated.
512 devices in a mesh: seq: 32 (over y, x), head: 16 (over z, core).
Axes of the slice: x: 4, y: 8, z: 8, core: 2. Of those that a mesh axis runs over, the one named last changes fastest.
Arguments:
- queries: bfloat16 [2048, 8192], P('seq', 'head'), may hold values from -6 to 6
- keys: bfloat16 [2048, 1024], P('seq'), may hold values from -6 to 6
- values: bfloat16 [2048, 1024], P('seq'), may hold values from -6 to 6
- vertical: int32 [64, 8], replicated, may hold values from -1 to 31, as said below
- slash: int32 [64, 8], replicated, may hold values from -1 to 31, as said below
- plan: int32 [64], replicated, may hold values from 0 to 63, each once
Outputs:
- attended: bfloat16 [2048, 8192], P('seq', 'head')
Inputs may be any that keep to these rules, and one draw needn't show every extreme that they name: `vertical`: entries of 0 or more name key blocks of 64 positions; -1 marks an unused entry, and every row has at least one used entry. `slash`: entries of 0 or more are offsets back from a query's own block; -1 marks an unused entry; the first entry of every row is 0. `plan`: A permutation of the query heads.
All inputs are finite; a program needn't handle non-finite values.
Results may differ from a plain program's by a relative error of at most 0.0044.
Values may be sent and summed in bfloat16 or wider, within the bound.
A program may use at most 64 MiB of HBM per device.

v0:
```python
import jax
import jax.numpy as jnp
from jax import lax
from jax.sharding import PartitionSpec as P

HD = 128
QH = 64
KVH = 8
BLK = 64
floor_value = -1e30


def block_mask(query_blocks, key_blocks, vertical_rows, slash_rows, query_pos, key_pos):
    vertical_hit = jnp.any(vertical_rows[:, :, None] == key_blocks[None, None, :], axis=1)
    distance = query_blocks[:, None] - key_blocks[None, :]
    slash_hit = jnp.zeros((slash_rows.shape[0],) + distance.shape, jnp.bool_)
    for column in range(slash_rows.shape[1]):
        slash_hit = slash_hit | (slash_rows[:, column][:, None, None] == distance[None])
    causal = key_pos[None, :] <= query_pos[:, None]
    return causal[None] & (vertical_hit[:, None, :] | slash_hit)


def attend(carried, query_group, key_group, value_group, allowed, score_scale):
    max_old, totals_old, sums_old = carried
    scores = (
        jnp.einsum("qgh,kgh->gqk", query_group, key_group, preferred_element_type=jnp.float32)
        * score_scale
    )
    masked = jnp.where(allowed, scores, floor_value)
    max_new = jnp.maximum(max_old, jnp.max(masked, axis=2))
    weights = jnp.exp(masked - max_new[:, :, None])
    totals_new = jnp.sum(weights, axis=2)
    mixture = jnp.einsum(
        "gqk,kgh->qgh",
        weights.astype(jnp.bfloat16),
        value_group,
        preferred_element_type=jnp.float32,
    )
    return (max_new, totals_new, mixture)


def per_device(queries, keys, values, vertical, slash, plan):
    slot_count = plan.shape[0] // lax.axis_size("head")
    query_len = queries.shape[0]
    key_len = keys.shape[0]
    group_size = QH // KVH
    my_heads = lax.dynamic_slice_in_dim(plan, lax.axis_index("head") * slot_count, slot_count)
    kv_index = my_heads // group_size
    slot_column = jnp.arange(slot_count, dtype=jnp.int32)
    key_pick = jnp.take(keys.reshape(key_len, KVH, HD), kv_index, axis=1).reshape(
        key_len, slot_count * HD
    )
    value_pick = jnp.take(values.reshape(key_len, KVH, HD), kv_index, axis=1).reshape(
        key_len, slot_count * HD
    )
    gathered = lax.all_gather(queries, "head", axis=1, tiled=True)
    query_sel = jnp.take(gathered.reshape(query_len, QH, HD), my_heads, axis=1)
    vertical_sel = jnp.take(vertical, my_heads, axis=0)
    slash_sel = jnp.take(slash, my_heads, axis=0)
    query_pos = lax.axis_index("seq") * query_len + jnp.arange(query_len, dtype=jnp.int32)
    query_blocks = query_pos // BLK
    score_scale = HD ** (-0.5)

    def select_rows(rows):
        return jnp.take(rows.reshape(rows.shape[0], slot_count, HD), slot_column, axis=1)

    initial = (
        jnp.full((slot_count, query_len), floor_value, jnp.float32),
        jnp.zeros((slot_count, query_len), jnp.float32),
        jnp.zeros((query_len, slot_count, HD), jnp.float32),
    )
    key_piece = select_rows(lax.all_gather(key_pick, "seq", axis=0, tiled=True))
    value_piece = select_rows(lax.all_gather(value_pick, "seq", axis=0, tiled=True))
    piece_len = key_piece.shape[0]
    key_pos = jnp.arange(piece_len, dtype=jnp.int32)
    allowed = block_mask(query_blocks, key_pos // BLK, vertical_sel, slash_sel, query_pos, key_pos)
    max_parts = []
    total_parts = []
    sum_parts = []
    for lead in range(0, slot_count, 2):
        previous = (
            initial[0][lead : lead + 2],
            initial[1][lead : lead + 2],
            initial[2][:, lead : lead + 2],
        )
        updated = attend(
            previous,
            query_sel[:, lead : lead + 2],
            key_piece[:, lead : lead + 2],
            value_piece[:, lead : lead + 2],
            allowed[lead : lead + 2],
            score_scale,
        )
        max_parts.append(updated[0])
        total_parts.append(updated[1])
        sum_parts.append(updated[2])
    output = (
        jnp.concatenate(sum_parts, axis=1)
        / jnp.transpose(jnp.concatenate(total_parts, axis=0))[:, :, None]
    )
    return output.reshape(query_len, slot_count * HD).astype(jnp.bfloat16)


def solution(mesh):
    in_specs = (P("seq", "head"), P("seq", None), P("seq", None), P(), P(), P())
    out_specs = P("seq", "head")
    return jax.shard_map(
        per_device, mesh=mesh, in_specs=in_specs, out_specs=out_specs, check_vma=False
    )
```

profile of v0, /device:TPU:16, one launch (start us, length us, event | category | flops | bytes accessed | tf_op | source)
XLA Modules:
  0.0 250.0 jit_solution(17985091205724103392)
XLA Ops:
  6.5 0.0 copy-start
  6.5 0.0 all-gather.6.cloned.1.call-start
  6.5 0.7 all-gather.6.cloned.1.call-update
  7.3 0.0 all-gather.4.cloned.1.call-start
  7.3 0.7 compare_and_fusion
  8.1 0.0 copy-done
  8.1 0.6 gather_fusion.5
  8.7 0.9 copy_bitcast_fusion.1
  9.6 0.6 gather_fusion.1
  10.2 0.1 select_bitcast_fusion.3
  10.3 0.6 copy.48
  10.9 0.0 all-gather.4.cloned.1.call-update
  10.9 0.0 all-gather.8.cloned.1.call-start
  11.0 0.6 copy.49
  11.6 0.0 all-gather.8.cloned.1.call-update
  11.7 0.8 copy.28
  12.4 0.8 copy.29
  13.2 0.6 gather_fusion.3
  13.8 0.6 gather_fusion.4
  14.4 0.1 broadcast_select_fusion.4
  14.5 0.3 slice_reduce_fusion.7
  14.8 0.2 compare_reduce_fusion
  14.9 0.1 iota_compare_fusion
  15.1 0.1 broadcast_subtract_fusion
  15.2 2.2 or_and_fusion
  17.4 38.6 %all-gather.6.cloned.1.call-done = bf16[64,8192]{1,0:T(8,128)(2,1)} async-done(((bf16[64,512]{1,0:T(8,128)(2,1)}), bf16[64,8192]{1,0:T(8,128)(2,1)}) %all-gather.6.cloned.1.call-update) | async-done | bytes 1048592 | tf_op jit(solution)/shard_map/all_gather | solution.py:56
  56.0 1.5 copy_bitcast_fusion
  57.5 0.6 gather_fusion
  58.1 82.0 %all-gather.4.cloned.1.call-done = bf16[2048,512]{1,0:T(8,128)(2,1)} async-done(((bf16[64,512]{1,0:T(8,128)(2,1)}), bf16[2048,512]{1,0:T(8,128)(2,1)}) %all-gather.4.cloned.1.call-update) | async-done | bytes 2097168 | tf_op jit(solution)/shard_map/all_gather | solution.py:73
  140.1 3.9 %copy.26 = bf16[2048,512]{0,1:T(8,128)(2,1)} copy(bf16[2048,512]{1,0:T(8,128)(2,1)} %all-gather.4.cloned.1.call-done) | data formatting | bytes 4194304 | tf_op jit(solution)/shard_map/all_gather | solution.py:73
  144.1 3.0 %copy.27 = bf16[2048,4,128]{2,0,1:T(8,128)(2,1)S(1)} copy(bf16[2048,4,128]{0,2,1:T(8,128)(2,1)} %bitcast.53) | data formatting | bytes 4194304 | tf_op jit(solution)/shard_map/reshape | solution.py:65
  147.1 76.9 %all-gather.8.cloned.1.call-done = bf16[2048,512]{1,0:T(8,128)(2,1)} async-done(((bf16[64,512]{1,0:T(8,128)(2,1)}), bf16[2048,512]{1,0:T(8,128)(2,1)}) %all-gather.8.cloned.1.call-update) | async-done | bytes 2097168 | tf_op jit(solution)/shard_map/all_gather | solution.py:72
  224.1 4.0 %copy.33 = bf16[2048,512]{0,1:T(8,128)(2,1)} copy(bf16[2048,512]{1,0:T(8,128)(2,1)} %all-gather.8.cloned.1.call-done) | data formatting | bytes 4194304 | tf_op jit(solution)/shard_map/all_gather | solution.py:72
  228.0 4.0 %copy.34 = bf16[2048,4,128]{2,0,1:T(8,128)(2,1)} copy(bf16[2048,4,128]{0,2,1:T(8,128)(2,1)} %bitcast.54) | data formatting | bytes 4194304 | tf_op jit(solution)/shard_map/reshape | solution.py:65
  232.0 2.1 gather_fusion.2
  234.1 0.0 copy-start.1
  234.1 3.9 %gather_fusion.6 = bf16[4,2048,128]{2,1,0:T(8,128)(2,1)} fusion(bf16[2048,4,128]{2,0,1:T(8,128)(2,1)} %copy.34, s32[1024]{0:T(1024)S(1)} %pad_clamp_fusion), kind=kCustom, calls=%fused_computation.4.clone | custom fusion | bytes 4194320 | tf_op jit(solution)/shard_map/jit(_take)/gather | solution.py:65
  238.0 0.0 copy-done.1
  238.0 2.0 select_bitcast_fusion.1
  240.0 0.6 fusion.23
  240.7 0.7 fusion.24
  241.3 0.3 fusion.8
  241.6 0.4 convolution_bitcast_fusion
  242.0 0.4 convolution_bitcast_fusion.1
  242.4 0.3 fusion.6
  242.8 0.7 copy_bitcast_fusion.3
  (11 shorter events, 0.1 us)
Async XLA Ops:
  6.5 1.5 copy-start
  6.5 49.5 %all-gather.6.cloned.1.call-start = ((), (), s32[]{:S(2)}) async-start(), calls=%async_computation.1 | async-start | bytes 1114112 | tf_op jit(solution)/shard_map/all_gather | solution.py:56
  7.3 132.9 %all-gather.4.cloned.1.call-start = ((), (), s32[]{:S(2)}) async-start(), calls=%async_computation | async-start | bytes 2162688 | tf_op jit(solution)/shard_map/all_gather | solution.py:73
  10.9 213.1 %all-gather.8.cloned.1.call-start = ((), (), s32[]{:S(2)}) async-start(), calls=%async_computation.2 | async-start | bytes 2162688 | tf_op jit(solution)/shard_map/all_gather | solution.py:72
  234.1 3.9 %copy-start.1 = (bf16[4,2048,128]{2,1,0:T(8,128)(2,1)S(1)}, bf16[4,2048,128]{2,1,0:T(8,128)(2,1)}, u32[]{:S(2)}) copy-start(bf16[4,2048,128]{2,1,0:T(8,128)(2,1)} %gather_fusion.2) | copy-start | bytes 6291460
Sparse Core Ops, SparseCore 0:
  9.5 46.4 all-gather.5
  59.2 80.8 all-gather.3
  143.3 80.7 all-gather.7
where the time goes:
time: 251 us; the launch traced here: 250 us
  waiting for transfers between devices  198 us (79%)
  local copies, waits for them, and re-layouts  29.3 us (12%)
  between operations  13.3 us (5%)
  other arithmetic  6.95 us (3%)
    all_gather x1, waiting for transfers between devices, per_device(): lax.all_gather(value_pick, 'seq', axis=0, tiled=True)  82 us
    all_gather x1, waiting for transfers between devices, per_device(): key_piece = select_rows(lax.all_gather(key_pick, 'seq', axis=0, tiled=True))  76.9 us
    all_gather x1, waiting for transfers between devices, per_device(): gathered = lax.all_gather(queries, 'head', axis=1, tiled=True)  38.6 us
    reshape x2, local copies, waits for them, and re-layouts, select_rows(): rows.reshape(rows.shape[0], slot_count, HD)  6.99 us
    gather x2, local copies, waits for them, and re-layouts, select_rows(): jnp.take(rows.reshape(rows.shape[0], slot_count, HD), slot_column, axis=1)  5.99 us
  transfers between devices with their start and end apart: 3, of which 3 were waited for; matrix products, arithmetic and copies ran while one was open for 8% of the time, Pallas kernels for 0%

commit v1 on v0

--- a/solution.py
+++ b/solution.py
@@ -53,7 +53,9 @@
     value_pick = jnp.take(values.reshape(key_len, KVH, HD), kv_index, axis=1).reshape(
         key_len, slot_count * HD
     )
-    gathered = lax.all_gather(queries, "head", axis=1, tiled=True)
+    gathered = jnp.concatenate(
+        lax.all_to_all(jnp.stack([queries] * lax.axis_size("head")), "head", 0, 0), axis=1
+    )
     query_sel = jnp.take(gathered.reshape(query_len, QH, HD), my_heads, axis=1)
     vertical_sel = jnp.take(vertical, my_heads, axis=0)
     slash_sel = jnp.take(slash, my_heads, axis=0)

time: 251 us -> 209 us (0.83)
  waiting for transfers between devices: 198 us -> 144 us
  starting transfers between devices: 0.08 us -> 10.5 us
    all_gather x1 -> x0, waiting for transfers between devices: 38.6 us -> none  [per_device(): gathered = lax.all_gather(queries, 'head', axis=1, tiled=True)]
    all_gather x1, waiting for transfers between devices: 82 us -> 45.1 us  [per_device(): lax.all_gather(value_pick, 'seq', axis=0, tiled=True)]
    all_to_all x0 -> x1, waiting for transfers between devices: none -> 22.3 us  [per_device(): lax.all_to_all(jnp.stack([queries] * lax.axis_size('head')), 'head', 0, 0)]
    all_to_all x0 -> x1, starting transfers between devices: none -> 10.4 us  [per_device(): lax.all_to_all(jnp.stack([queries] * lax.axis_size('head')), 'head', 0, 0)]
    another operation x0 -> x3, local copies, waits for them, and re-layouts: none -> 3.27 us  [the longest x1 1.92 us: per_device(): jnp.stack([queries] * lax.axis_size('head'))]
where the time goes in v1:
time: 209 us
  waiting for transfers between devices  144 us (69%)
  local copies, waits for them, and re-layouts  31.1 us (15%)
  between operations  13.6 us (7%)
  starting transfers between devices  10.5 us (5%)
  other arithmetic  6.95 us (3%)
    all_gather x1, waiting for transfers between devices, per_device(): key_piece = select_rows(lax.all_gather(key_pick, 'seq', axis=0, tiled=True))  76.9 us
    all_gather x1, waiting for transfers between devices, per_device(): lax.all_gather(value_pick, 'seq', axis=0, tiled=True)  45.1 us
    all_to_all x1, waiting for transfers between devices, per_device(): lax.all_to_all(jnp.stack([queries] * lax.axis_size('head')), 'head', 0, 0)  22.3 us
    all_to_all x1, starting transfers between devices, per_device(): lax.all_to_all(jnp.stack([queries] * lax.axis_size('head')), 'head', 0, 0)  10.4 us
    reshape x2, local copies, waits for them, and re-layouts, select_rows(): rows.reshape(rows.shape[0], slot_count, HD)  6.99 us
    gather x2, local copies, waits for them, and re-layouts, select_rows(): jnp.take(rows.reshape(rows.shape[0], slot_count, HD), slot_column, axis=1)  5.99 us
  transfers between devices with their start and end apart: 3, of which 3 were waited for; matrix products, arithmetic and copies ran while one was open for 8% of the time, Pallas kernels for 0%

profile of v1, /device:TPU:16, one launch (start us, length us, event | category | flops | bytes accessed | tf_op | source)
XLA Modules:
  0.0 208.7 jit_solution(12668821328732007236)
XLA Ops:
  6.5 0.0 all-gather.3.cloned.1.call-start
  6.5 0.9 copy-done
  7.5 0.9 copy_bitcast_fusion
  8.4 0.0 copy-start.2
  8.4 0.7 compare_and_fusion
  9.2 0.0 copy-start.3
  9.2 0.6 gather_fusion.5
  9.8 0.6 gather_fusion.1
  10.3 0.1 select_bitcast_fusion.3
  10.4 0.6 copy.61
  11.1 0.0 all-gather.3.cloned.1.call-update
  11.1 0.0 all-gather.5.cloned.1.call-start
  11.1 0.6 copy.62
  11.8 0.1 all-gather.5.cloned.1.call-update
  11.8 1.9 stack.2
  13.7 10.4 %all-to-all-start = ((bf16[16,64,512]{2,1,0:T(8,128)(2,1)}), bf16[16,64,512]{2,1,0:T(8,128)(2,1)S(1)}, u32[]{:S(2)}, u32[]{:S(2)}) async-start(bf16[16,64,512]{2,1,0:T(8,128)(2,1)} %stack.2), calls=%async_computation | async-start | bytes 2097152 | tf_op jit(solution)/shard_map/all_to_all | solution.py:57
  24.2 0.0 copy-done.2
  24.2 0.1 copy.42
  24.3 0.1 copy.43
  24.4 0.6 gather_fusion.3
  24.9 0.6 gather_fusion.4
  25.5 0.1 broadcast_select_fusion.4
  25.6 0.3 slice_reduce_fusion.7
  25.9 0.2 compare_reduce_fusion
  26.1 0.1 iota_compare_fusion
  26.2 0.1 broadcast_subtract_fusion
  26.3 2.2 %or_and_fusion = pred[4,64,2048]{2,1,0:T(32,128)(4,1)S(1)} fusion(s32[64,2048]{1,0:T(8,128)S(1)} %broadcast_subtract_fusion, s32[4]{0:T(128)S(1)} %get-tuple-element.8, s32[4]{0:T(128)S(1)} %get-tuple-element.10, s32[4]{0:T(128)S(1)} %get-tuple-element.11, s32[4]{0:T(128)S(1)} %get-tuple-element.12, s32[4]{0:T(128)S(1)} %get-tuple-element.13, ...), kind=kLoop, calls=%fused_computation.13 | loop fusion | flops 8912896 | bytes 1187968 | tf_op jit(solution)/shard_map/and | solution.py:20
  28.6 22.3 %all-to-all-done = bf16[16,64,512]{2,1,0:T(8,128)(2,1)S(1)} async-done(((bf16[16,64,512]{2,1,0:T(8,128)(2,1)}), bf16[16,64,512]{2,1,0:T(8,128)(2,1)S(1)}, u32[]{:S(2)}, u32[]{:S(2)}) %all-to-all-start) | async-done | bytes 1048608 | tf_op jit(solution)/shard_map/all_to_all | solution.py:57
  50.8 0.6 copy.44
  51.4 0.7 reshape_reshape.3
  52.1 0.7 copy.45
  52.8 0.6 gather_fusion
  53.3 45.1 %all-gather.3.cloned.1.call-done = bf16[2048,512]{1,0:T(8,128)(2,1)} async-done(((bf16[64,512]{1,0:T(8,128)(2,1)}), bf16[2048,512]{1,0:T(8,128)(2,1)}) %all-gather.3.cloned.1.call-update) | async-done | bytes 2097168 | tf_op jit(solution)/shard_map/all_gather | solution.py:75
  98.5 3.9 %copy.40 = bf16[2048,512]{0,1:T(8,128)(2,1)} copy(bf16[2048,512]{1,0:T(8,128)(2,1)} %all-gather.3.cloned.1.call-done) | data formatting | bytes 4194304 | tf_op jit(solution)/shard_map/all_gather | solution.py:75
  102.4 3.0 %copy.41 = bf16[2048,4,128]{2,0,1:T(8,128)(2,1)S(1)} copy(bf16[2048,4,128]{0,2,1:T(8,128)(2,1)} %bitcast.49) | data formatting | bytes 4194304 | tf_op jit(solution)/shard_map/reshape | solution.py:67
  105.5 76.9 %all-gather.5.cloned.1.call-done = bf16[2048,512]{1,0:T(8,128)(2,1)} async-done(((bf16[64,512]{1,0:T(8,128)(2,1)}), bf16[2048,512]{1,0:T(8,128)(2,1)}) %all-gather.5.cloned.1.call-update) | async-done | bytes 2097168 | tf_op jit(solution)/shard_map/all_gather | solution.py:74
  182.4 4.0 %copy.48 = bf16[2048,512]{0,1:T(8,128)(2,1)} copy(bf16[2048,512]{1,0:T(8,128)(2,1)} %all-gather.5.cloned.1.call-done) | data formatting | bytes 4194304 | tf_op jit(solution)/shard_map/all_gather | solution.py:74
  186.4 4.0 %copy.49 = bf16[2048,4,128]{2,0,1:T(8,128)(2,1)} copy(bf16[2048,4,128]{0,2,1:T(8,128)(2,1)} %bitcast.50) | data formatting | bytes 4194304 | tf_op jit(solution)/shard_map/reshape | solution.py:67
  190.3 2.1 %gather_fusion.2 = bf16[4,2048,128]{2,1,0:T(8,128)(2,1)} fusion(bf16[2048,4,128]{2,0,1:T(8,128)(2,1)S(1)} %copy.41, s32[1024]{0:T(1024)S(1)} %pad_clamp_fusion), kind=kCustom, calls=%fused_computation.1.clone | custom fusion | bytes 4194320 | tf_op jit(solution)/shard_map/jit(_take)/gather | solution.py:67
  192.4 3.9 %gather_fusion.6 = bf16[4,2048,128]{2,1,0:T(8,128)(2,1)} fusion(bf16[2048,4,128]{2,0,1:T(8,128)(2,1)} %copy.49, s32[1024]{0:T(1024)S(1)} %pad_clamp_fusion), kind=kCustom, calls=%fused_computation.4.clone | custom fusion | bytes 4194320 | tf_op jit(solution)/shard_map/jit(_take)/gather | solution.py:67
  196.3 2.0 select_bitcast_fusion.1
  198.4 0.6 fusion.23
  199.0 0.7 fusion.24
  199.7 0.3 fusion.8
  200.0 0.4 convolution_bitcast_fusion
  200.4 0.4 convolution_bitcast_fusion.1
  200.8 0.3 fusion.6
  201.1 0.7 copy_bitcast_fusion.2
  (14 shorter events, 0.1 us)
Async XLA Ops:
  6.5 0.9 copy-start
  6.5 92.0 %all-gather.3.cloned.1.call-start = ((), (), s32[]{:S(2)}) async-start(), calls=%async_computation.1 | async-start | bytes 2162688 | tf_op jit(solution)/shard_map/all_gather | solution.py:75
  8.4 15.8 %copy-start.2 = (s32[64,8]{0,1:T(8,128)S(1)}, s32[64,8]{0,1:T(8,128)}, u32[]{:S(2)}) copy-start(s32[64,8]{0,1:T(8,128)} %param.15) | copy-start | bytes 6148
  9.2 15.1 %copy-start.3 = (s32[64,8]{0,1:T(8,128)S(1)}, s32[64,8]{0,1:T(8,128)}, u32[]{:S(2)}) copy-start(s32[64,8]{0,1:T(8,128)} %param.16) | copy-start | bytes 6148
  11.1 171.3 %all-gather.5.cloned.1.call-start = ((), (), s32[]{:S(2)}) async-start(), calls=%async_computation.2 | async-start | bytes 2162688 | tf_op jit(solution)/shard_map/all_gather | solution.py:74
  13.7 37.1 %all-to-all-start = ((bf16[16,64,512]{2,1,0:T(8,128)(2,1)}), bf16[16,64,512]{2,1,0:T(8,128)(2,1)S(1)}, u32[]{:S(2)}, u32[]{:S(2)}) async-start(bf16[16,64,512]{2,1,0:T(8,128)(2,1)} %stack.2), calls=%async_computation | async-start | bytes 2097152 | tf_op jit(solution)/shard_map/all_to_all | solution.py:57
  192.4 3.9 %copy-start.1 = (bf16[4,2048,128]{2,1,0:T(8,128)(2,1)S(1)}, bf16[4,2048,128]{2,1,0:T(8,128)(2,1)}, u32[]{:S(2)}) copy-start(bf16[4,2048,128]{2,1,0:T(8,128)(2,1)} %gather_fusion.2) | copy-start | bytes 6291460
Sparse Core Ops, SparseCore 0:
  11.2 87.2 all-gather.2
  101.7 80.7 all-gather.4
